TPU v7x, 32 devices: a whole 2x2x4 slice. The times are simulated.
32 devices in a mesh: groups: 2 (over y), fib: 4 (over z), col: 4 (over x, core).
Axes of the slice: x: 2, y: 2, z: 4, core: 2. Of those that a mesh axis runs over, the one named last changes fastest.
Arguments:
- data_slab: float32 [256, 256, 2048], P(('groups', 'fib'), 'col'), parts along dimension 0, may hold values from -6 to 6
- first_factor: float32 [128, 96], replicated, may hold values from -0.5 to 0.5
- second_factor: float32 [256, 96], replicated, may hold values from -0.375 to 0.375
Outputs:
- core_slab: float32 [192, 96, 2048], P(('groups', 'col'), None, 'fib'), parts along dimension 0
There are 2 independent parts, one for each index of `groups`. A program takes and returns all parts, laid end to end along the dimension named above; an argument that names none is the same for every part. Nothing has to cross between parts.
All inputs are finite; a program needn't handle non-finite values.
Results may differ from a plain program's by a relative error of at most 0.00007.
Values sent between devices are 32-bit elements; how exact they have to be, the bound alone decides.
A program may use at most 256 MiB of HBM per device.

v0:
```python
import jax
import jax.numpy as jnp
from jax import lax
from jax.sharding import PartitionSpec as P


def second_mode(first_core, second_factor):
    return jnp.einsum(
        "jq,rjc->rqc",
        second_factor,
        lax.all_to_all(first_core, "col", split_axis=0, concat_axis=1, tiled=True),
        precision=lax.Precision.HIGHEST,
    )


def on_device(data_slab, first_factor, second_factor):
    moved_slab = lax.all_to_all(data_slab, "fib", split_axis=2, concat_axis=0, tiled=True)
    first_core = jnp.einsum(
        "ir,ijc->rjc", first_factor, moved_slab, precision=lax.Precision.HIGHEST
    )
    return second_mode(first_core, second_factor)


def solution(mesh):
    in_specs = (P(("groups", "fib"), "col", None), P(), P())
    out_specs = P(("groups", "col"), None, "fib")
    return jax.shard_map(
        on_device, mesh=mesh, in_specs=in_specs, out_specs=out_specs, check_vma=False
    )
```

profile of v0, /device:TPU:1, one launch (start us, length us, event | category | flops | bytes accessed | tf_op | source)
XLA Modules:
  0.0 791.0 jit_solution(12158534761154474042)
XLA Ops:
  0.0 0.0 copy-start
  0.0 30.5 %copy.6 = f32[32,64,2048]{1,0,2:T(8,128)} copy(f32[32,64,2048]{2,1,0:T(8,128)} %param.3) | data formatting | bytes 33554432 | tf_op args[0]
  30.5 42.1 %reshape.2 = f32[4,1,1048576]{2,1,0:T(1,128)} reshape(f32[2048,32,64]{2,1,0:T(8,128)} %bitcast.21) | data formatting | bytes 33554432
  72.5 374.4 %all_to_all.36 = f32[4,1,1048576]{2,1,0:T(1,128)} all-to-all(f32[4,1,1048576]{2,1,0:T(1,128)} %reshape.2), channel_id=1, replica_groups=mesh['groups'=2,'fib'=4,'col'=4] {'fib'}, dimensions={0} | all-to-all | bytes 33554432 | tf_op jit(solution)/shard_map/all_to_all | solution.py:17
  447.0 0.5 broadcast
  447.5 54.5 %reduce = f32[4,1048576]{1,0:T(4,128)} reduce(f32[4,1,1048576]{2,1,0:T(1,128)} %all_to_all.36, f32[]{:T(128)} %broadcast), dimensions={1}, to_apply=%all_to_all.26.reduce_sub_computation | reduce | bytes 33554436 | tf_op jit(solution)/shard_map/all_to_all | solution.py:17
  501.9 55.1 %reshape.3 = f32[2048,32,64]{2,1,0:T(8,128)} reshape(f32[4,1048576]{1,0:T(4,128)} %reduce) | data formatting | bytes 33554432
  557.1 0.0 copy-start.1
  557.1 26.2 %copy.7 = f32[32,64,4,512]{3,0,2,1:T(8,128)} copy(f32[32,64,4,512]{1,0,3,2:T(8,128)} %bitcast.20) | data formatting | bytes 33554432 | tf_op jit(solution)/shard_map/all_to_all | solution.py:17
  583.3 0.0 copy-done.1
  583.3 19.0 %fusion.1 = f32[96,64,512]{2,0,1:T(8,128)} fusion(f32[128,64,512]{2,0,1:T(8,128)} %bitcast.22, f32[128,96]{0,1:T(8,128)S(1)} %copy-done.1), kind=kOutput, calls=%fused_computation.2 | convolution fusion | flops 4831838208 | bytes 29409280 | tf_op jit(solution)/shard_map/ir,ijc->rjc/dot_general | solution.py:18
  602.3 16.3 %copy.8 = f32[96,64,512]{2,1,0:T(8,128)} copy(f32[96,64,512]{2,0,1:T(8,128)} %fusion.1) | data formatting | bytes 25165824 | tf_op jit(solution)/shard_map/ir,ijc->rjc/dot_general | solution.py:18
  618.7 147.9 %all_to_all.37 = f32[96,64,512]{2,1,0:T(8,128)} all-to-all(f32[96,64,512]{2,1,0:T(8,128)} %copy.8), channel_id=1, replica_groups=mesh['groups'=2,'fib'=4,'col'=4] {'col'}, dimensions={0} | all-to-all | bytes 25165824 | tf_op jit(solution)/shard_map/all_to_all | solution.py:11
  766.5 11.9 %copy.9 = f32[4,24,64,512]{3,2,0,1:T(8,128)} copy(f32[4,24,64,512]{3,2,1,0:T(8,128)} %bitcast.23) | data formatting | bytes 25165824 | tf_op jit(solution)/shard_map/all_to_all | solution.py:11
  778.4 0.0 copy-done
  778.4 12.0 %convolution_bitcast_fusion = f32[24,96,512]{2,1,0:T(8,128)} fusion(f32[24,256,512]{2,1,0:T(8,128)} %bitcast.24, f32[256,96]{0,1:T(8,128)S(1)} %copy-done), kind=kOutput, calls=%fused_computation | convolution fusion | flops 3623878656 | bytes 17399808 | tf_op jit(solution)/shard_map/jq,rjc->rqc/dot_general | solution.py:8
Async XLA Ops:
  0.0 778.4 %copy-start = (f32[256,96]{0,1:T(8,128)S(1)}, f32[256,96]{0,1:T(8,128)}, u32[]{:S(2)}) copy-start(f32[256,96]{0,1:T(8,128)} %param.5) | copy-start | bytes 294916
  557.1 26.2 %copy-start.1 = (f32[128,96]{0,1:T(8,128)S(1)}, f32[128,96]{0,1:T(8,128)}, u32[]{:S(2)}) copy-start(f32[128,96]{0,1:T(8,128)} %param.4) | copy-start | bytes 147460
where the time goes:
time: 801 us; the launch traced here: 791 us
  blocking collectives  522 us (65%)
  local copies, waits for them, and re-layouts  183 us (23%)
  other arithmetic  54.5 us (7%)
  matrix products  31.1 us (4%)
    all_to_all x1, blocking collectives, on_device(): lax.all_to_all(data_slab, 'fib', split_axis=2, concat_axis=0, tiled=True)  374 us
    all_to_all x1, blocking collectives, second_mode(): lax.all_to_all(first_core, 'col', split_axis=0, concat_axis=1, tiled=True)  148 us
    unnamed x7, local copies, waits for them, and re-layouts  128 us
    all_to_all x1, other arithmetic, on_device(): lax.all_to_all(data_slab, 'fib', split_axis=2, concat_axis=0, tiled=True)  54.5 us
    all_to_all x2, local copies, waits for them, and re-layouts, on_device(): lax.all_to_all(data_slab, 'fib', split_axis=2, concat_axis=0, tiled=True)  26.7 us
    dot_general x1, matrix products, on_device(): jnp.einsum('ir,ijc->rjc', first_factor, moved_slab, precision=lax.Precisi...  19 us
    dot_general x1, local copies, waits for them, and re-layouts, on_device(): jnp.einsum('ir,ijc->rjc', first_factor, moved_slab, precision=lax.Precisi...  16.3 us

commit v1 on v0

--- a/solution.py
+++ b/solution.py
@@ -1,7 +1,18 @@
+import functools
+
 import jax
 import jax.numpy as jnp
 from jax import lax
+from jax.experimental import pallas as pl
+from jax.experimental.pallas import tpu as pltpu
 from jax.sharding import PartitionSpec as P
+
+MESH = pl.DeviceIdType.MESH
+LANES = 128
+Q_CHUNKS = 3
+I_CHUNKS = 8
+LAG = 2
+OUT_LAG = 2
 
 
 def second_mode(first_core, second_factor):
@@ -21,9 +32,252 @@
     return second_mode(first_core, second_factor)
 
 
+def split(values):
+    high = values.astype(jnp.bfloat16)
+    low = (values - high.astype(jnp.float32)).astype(jnp.bfloat16)
+    return high, low
+
+
+def kernel(
+    nz, nq, ni, slab, f1, f2, out, xcat, pb, xr, g, rr, a1, a2,
+    core_send, core_recv, core_local, x_send, x_recv, z_send, z_recv, o_send, o_recv, o_local,
+):
+    rows, jl, _ = slab.shape
+    ic_rows = rows // ni
+    qc_rows = pb.shape[4]
+    ranks = f1.shape[1]
+    own_ranks = out.shape[0]
+    z = lax.axis_index("fib")
+    k = lax.axis_index("col")
+    x, core = k // 2, lax.rem(k, 2)
+    sibling = 2 * x + (1 - core)
+    partner = 2 * (1 - x) + core
+
+    barrier = pltpu.get_barrier_semaphore()
+    for e in range(1, 4):
+        pl.semaphore_signal(
+            barrier, inc=1, device_id={"col": lax.rem(k + e, 4)}, device_id_type=MESH
+        )
+    for d in range(1, nz):
+        pl.semaphore_signal(
+            barrier, inc=1, device_id={"fib": lax.rem(z + d, nz)}, device_id_type=MESH
+        )
+    pl.semaphore_wait(barrier, 3 + nz - 1)
+
+    def wait(ref, sem):
+        pltpu.make_async_copy(ref, ref, sem).wait()
+
+    my_j = pl.ds(pl.multiple_of(core * jl, jl), jl)
+    their_j = pl.ds(pl.multiple_of((1 - core) * jl, jl), jl)
+
+    @pl.loop(0, ni)
+    def _(ic):
+        chunk = pl.ds(ic * ic_rows, ic_rows)
+        for zi in range(nz):
+            base = zi * 4 * LANES
+            cells = pl.ds(zi * 2 * LANES, 2 * LANES)
+            theirs = pl.ds(pl.multiple_of(base + (1 - core) * 2 * LANES, 2 * LANES), 2 * LANES)
+            mine = pl.ds(pl.multiple_of(base + core * 2 * LANES, 2 * LANES), 2 * LANES)
+            pltpu.make_async_remote_copy(
+                src_ref=slab.at[chunk, :, theirs],
+                dst_ref=xcat.at[chunk, my_j, cells],
+                send_sem=core_send.at[ic],
+                recv_sem=core_recv.at[ic],
+                device_id={"col": sibling},
+                device_id_type=MESH,
+            ).start()
+            pltpu.make_async_copy(
+                slab.at[chunk, :, mine], xcat.at[chunk, my_j, cells], core_local.at[ic]
+            ).start()
+
+    def place(ref, factor, size):
+        high, low = split(factor)
+        depth = factor.shape[1]
+        for qc in range(ref.shape[0]):
+            at = slice(qc * size, (qc + 1) * size)
+            ref[qc, :size, :depth] = high[at]
+            ref[qc, :size, depth:] = high[at]
+            ref[qc, size:, :depth] = low[at]
+            ref[qc, size:, depth:] = jnp.zeros_like(low[at])
+
+    place(a2, f2[pl.ds(pl.multiple_of(x * 2 * jl, 2 * jl), 2 * jl), :].T, qc_rows)
+    place(a1, f1[...].T, ranks)
+
+    def product(factor, values):
+        high, low = split(values)
+        both = jnp.dot(
+            factor, jnp.concatenate([high, low], axis=0), preferred_element_type=jnp.float32
+        )
+        half = both.shape[0] // 2
+        return both[:half] + both[half:]
+
+    def to_second_rank(s):
+        qc, ic = s // ni, lax.rem(s, ni)
+        chunk = pl.ds(ic * ic_rows, ic_rows)
+
+        @pl.when(qc == 0)
+        def _():
+            wait(xcat.at[chunk, my_j], core_local.at[ic])
+            wait(xcat.at[chunk, their_j], core_recv.at[ic])
+
+        @pl.loop(0, ic_rows)
+        def _(step):
+            i = ic * ic_rows + step
+            for zi in range(nz):
+                part = product(a2[qc], xcat[i, :, zi * 2 * LANES : (zi + 1) * 2 * LANES])
+                pb[0, qc, zi, i] = part[:, :LANES]
+                pb[1, qc, zi, i] = part[:, LANES:]
+
+        pltpu.make_async_remote_copy(
+            src_ref=pb.at[1 - x, qc, :, chunk],
+            dst_ref=xr.at[qc, :, chunk],
+            send_sem=x_send.at[s],
+            recv_sem=x_recv.at[s],
+            device_id={"col": partner},
+            device_id_type=MESH,
+        ).start()
+
+    def add_and_send(s):
+        qc, ic = s // ni, lax.rem(s, ni)
+        chunk = pl.ds(ic * ic_rows, ic_rows)
+        wait(xr.at[qc, :, chunk], x_recv.at[s])
+        for zi in range(nz):
+            pb[x, qc, zi, chunk] = pb[x, qc, zi, chunk] + xr[qc, zi, chunk]
+        g[qc, z, chunk] = pb[x, qc, z, chunk]
+        for d in range(1, nz):
+            peer = lax.rem(z + d, nz)
+            pltpu.make_async_remote_copy(
+                src_ref=pb.at[x, qc, peer, chunk],
+                dst_ref=g.at[qc, z, chunk],
+                send_sem=z_send.at[qc, d - 1],
+                recv_sem=z_recv.at[qc, d - 1],
+                device_id={"fib": peer},
+                device_id_type=MESH,
+            ).start()
+
+    def sub(column):
+        start = (lax.rem(column, 2) * 2 + column // 2) * LANES
+        return pl.ds(pl.multiple_of(start, LANES), LANES)
+
+    def to_first_rank(qc):
+        for d in range(1, nz):
+            wait(g.at[qc, lax.rem(z - d + nz, nz)], z_recv.at[qc, d - 1])
+        points = nz * rows
+        flat = g.at[qc].reshape(points * qc_rows, LANES)
+        ranked = rr.at[qc].reshape(ranks * qc_rows, LANES)
+
+        @pl.loop(0, qc_rows // 2)
+        def _(pair):
+            q = 2 * pair
+            values = jnp.concatenate(
+                [flat[pl.ds(q + t, points, stride=qc_rows), :] for t in range(2)], axis=1
+            )
+            part = product(a1[0], values)
+            for t in range(2):
+                ranked[pl.ds(q + t, ranks, stride=qc_rows), :] = part[
+                    :, t * LANES : (t + 1) * LANES
+                ]
+
+        qs = pl.ds(pl.multiple_of(qc * qc_rows, qc_rows), qc_rows)
+        for e in range(1, 4):
+            peer = lax.rem(k + e, 4)
+            pltpu.make_async_remote_copy(
+                src_ref=rr.at[qc, pl.ds(peer * own_ranks, own_ranks)],
+                dst_ref=out.at[:, qs, sub(k)],
+                send_sem=o_send.at[qc, e - 1],
+                recv_sem=o_recv.at[qc, e - 1],
+                device_id={"col": peer},
+                device_id_type=MESH,
+            ).start()
+        pltpu.make_async_copy(
+            rr.at[qc, pl.ds(k * own_ranks, own_ranks)], out.at[:, qs, sub(k)], o_local.at[qc]
+        ).start()
+
+    steps = nq * ni
+
+    @pl.loop(0, steps + LAG + OUT_LAG)
+    def _(s):
+        @pl.when(s < steps)
+        def _():
+            to_second_rank(s)
+
+        @pl.when((s >= LAG) & (s < steps + LAG))
+        def _():
+            add_and_send(s - LAG)
+
+        done = s - (LAG + OUT_LAG) + 1
+
+        @pl.when((done > 0) & (lax.rem(done, ni) == 0))
+        def _():
+            to_first_rank(done // ni - 1)
+
+    @pl.loop(0, ni)
+    def _(ic):
+        chunk = pl.ds(ic * ic_rows, ic_rows)
+        wait(xcat.at[chunk, my_j], core_send.at[ic])
+
+    @pl.loop(0, steps)
+    def _(s):
+        qc, ic = s // ni, lax.rem(s, ni)
+        wait(pb.at[1 - x, qc, :, pl.ds(ic * ic_rows, ic_rows)], x_send.at[s])
+
+    for qc in range(nq):
+        qs = pl.ds(qc * qc_rows, qc_rows)
+        for d in range(1, nz):
+            wait(pb.at[x, qc, lax.rem(z + d, nz)], z_send.at[qc, d - 1])
+        for e in range(1, 4):
+            wait(rr.at[qc, pl.ds(lax.rem(k + e, 4) * own_ranks, own_ranks)], o_send.at[qc, e - 1])
+            wait(out.at[:, qs, sub(lax.rem(k - e + 4, 4))], o_recv.at[qc, e - 1])
+        wait(out.at[:, qs, sub(k)], o_local.at[qc])
+
+
+def fused(nz, data_slab, first_factor, second_factor):
+    rows, jl, cells = data_slab.shape
+    ranks, qs = first_factor.shape[1], second_factor.shape[1]
+    nq, ni = Q_CHUNKS, I_CHUNKS
+    qc_rows = qs // nq
+    f32, bf16 = jnp.float32, jnp.bfloat16
+    dma = pltpu.SemaphoreType.DMA
+    scratch = [
+        pltpu.VMEM((rows, 2 * jl, cells // 2), f32),
+        pltpu.VMEM((2, nq, nz, rows, qc_rows, LANES), f32),
+        pltpu.VMEM((nq, nz, rows, qc_rows, LANES), f32),
+        pltpu.VMEM((nq, nz, rows, qc_rows, LANES), f32),
+        pltpu.VMEM((nq, ranks, qc_rows, LANES), f32),
+        pltpu.VMEM((1, 2 * ranks, 2 * nz * rows), bf16),
+        pltpu.VMEM((nq, 2 * qc_rows, 4 * jl), bf16),
+        dma((ni,)), dma((ni,)), dma((ni,)),
+        dma((nq * ni,)), dma((nq * ni,)),
+        dma((nq, nz - 1)), dma((nq, nz - 1)),
+        dma((nq, 3)), dma((nq, 3)), dma((nq,)),
+    ]
+    return pl.pallas_call(
+        functools.partial(kernel, nz, nq, ni),
+        out_shape=jax.ShapeDtypeStruct((ranks // 4, qs, cells // nz), f32),
+        in_specs=[
+            pl.BlockSpec(memory_space=pl.ANY),
+            pl.BlockSpec(memory_space=pltpu.VMEM),
+            pl.BlockSpec(memory_space=pltpu.VMEM),
+        ],
+        out_specs=pl.BlockSpec(memory_space=pl.ANY),
+        scratch_shapes=scratch,
+        compiler_params=pltpu.CompilerParams(
+            collective_id=0, has_side_effects=True, vmem_limit_bytes=56 * 1024 * 1024
+        ),
+    )(data_slab, first_factor, second_factor)
+
+
 def solution(mesh):
+    nz, nc = mesh.shape["fib"], mesh.shape["col"]
+
+    def on_each(data_slab, first_factor, second_factor):
+        cells = data_slab.shape[2]
+        if nc == 4 and nz > 1 and cells == nz * nc * LANES:
+            return fused(nz, data_slab, first_factor, second_factor)
+        return on_device(data_slab, first_factor, second_factor)
+
     in_specs = (P(("groups", "fib"), "col", None), P(), P())
     out_specs = P(("groups", "col"), None, "fib")
     return jax.shard_map(
-        on_device, mesh=mesh, in_specs=in_specs, out_specs=out_specs, check_vma=False
+        on_each, mesh=mesh, in_specs=in_specs, out_specs=out_specs, check_vma=False
     )

time: 801 us -> 218 us (0.27); the launches traced: 791 us -> 217 us
  blocking collectives: 522 us -> 0 us
  Pallas kernels: 0 us -> 209 us
  local copies, waits for them, and re-layouts: 183 us -> 8.46 us
  other arithmetic: 54.5 us -> 0 us
  matrix products: 31.1 us -> 0 us
    all_to_all x2 -> x0, blocking collectives: 522 us -> none  [the longest x1 374 us: on_device(): lax.all_to_all(data_slab, 'fib', split_axis=2, concat_axis=0, tiled=True)]
    pallas_call x0 -> x1, Pallas kernels: none -> 209 us  [fused(): pl.pallas_call(functools.partial(kernel, nz, nq, ni), out_shape=jax.Shape...]
    unnamed x7 -> x3, local copies, waits for them, and re-layouts: 128 us -> 8.46 us
    all_to_all x1 -> x0, other arithmetic: 54.5 us -> none  [on_device(): lax.all_to_all(data_slab, 'fib', split_axis=2, concat_axis=0, tiled=True)]
    all_to_all x3 -> x0, local copies, waits for them, and re-layouts: 38.6 us -> none  [the longest x2 26.7 us: on_device(): lax.all_to_all(data_slab, 'fib', split_axis=2, concat_axis=0, tiled=True)]
    dot_general x2 -> x0, matrix products: 31.1 us -> none  [the longest x1 19 us: on_device(): jnp.einsum('ir,ijc->rjc', first_factor, moved_slab, precision=lax.Precisi...]
    dot_general x1 -> x0, local copies, waits for them, and re-layouts: 16.3 us -> none  [on_device(): jnp.einsum('ir,ijc->rjc', first_factor, moved_slab, precision=lax.Precisi...]
where the time goes in v1:
time: 218 us; the launch traced here: 217 us
  Pallas kernels  209 us (96%)
  local copies, waits for them, and re-layouts  8.46 us (4%)
    pallas_call x1, Pallas kernels, fused(): pl.pallas_call(functools.partial(kernel, nz, nq, ni), out_shape=jax.Shape...  209 us
    unnamed x3, local copies, waits for them, and re-layouts  8.46 us

profile of v1, /device:TPU:1, one launch (start us, length us, event | category | flops | bytes accessed | tf_op | source)
XLA Modules:
  0.0 217.3 jit_solution(10532227822751050305)
XLA Ops:
  0.0 1.5 copy.4.f1
  1.5 1.6 copy.5.f2
  3.2 208.8 %shard_map.37 = f32[24,96,512]{2,1,0:T(8,128)} custom-call(f32[32,64,2048]{2,1,0:T(8,128)} %slab.1, f32[128,96]{1,0:T(8,128)} %copy.4.f1, f32[256,96]{1,0:T(8,128)} %copy.5.f2), custom_call_target="tpu_custom_call" | custom-call | tf_op jit(solution)/shard_map/pallas_call | solution.py:254
  212.0 5.3 %copy.7 = f32[24,96,512]{2,1,0:T(8,128)} copy(f32[24,96,512]{2,1,0:T(8,128)} %shard_map.37) | data formatting | bytes 9437184

commit v2 on v1

v2 whole, which is shorter than its diff:
```python
import functools

import jax
import jax.numpy as jnp
from jax import lax
from jax.experimental import pallas as pl
from jax.experimental.pallas import tpu as pltpu
from jax.sharding import PartitionSpec as P

MESH = pl.DeviceIdType.MESH
LANES = 128
Q_CHUNKS = 6
I_CHUNKS = 4
LAG = 2
VMEM_MIB = 50


def second_mode(first_core, second_factor):
    return jnp.einsum(
        "jq,rjc->rqc",
        second_factor,
        lax.all_to_all(first_core, "col", split_axis=0, concat_axis=1, tiled=True),
        precision=lax.Precision.HIGHEST,
    )


def on_device(data_slab, first_factor, second_factor):
    moved_slab = lax.all_to_all(data_slab, "fib", split_axis=2, concat_axis=0, tiled=True)
    first_core = jnp.einsum(
        "ir,ijc->rjc", first_factor, moved_slab, precision=lax.Precision.HIGHEST
    )
    return second_mode(first_core, second_factor)


def split(values):
    high = values.astype(jnp.bfloat16)
    low = (values - high.astype(jnp.float32)).astype(jnp.bfloat16)
    return high, low


def kernel(
    nz, nq, ni, slab, f1, f2, out, xcat, pb, xr, g, gf, rr, rf, rx, a1, a2,
    core_send, core_recv, core_local, x_send, x_recv, z_send, z_recv, zf_send, zf_recv,
    o_send, o_recv, o_local, f_send, f_recv, s_send, s_recv, s_local,
):
    rows, jl, _ = slab.shape
    ic_rows = rows // ni
    qc_rows = pb.shape[4]
    ranks = f1.shape[0]
    own_ranks = out.shape[0]
    points = nz * rows
    last = nq - 1
    z = lax.axis_index("fib")
    k = lax.axis_index("col")
    x, core = k // 2, lax.rem(k, 2)
    sibling = 2 * x + (1 - core)
    partner = 2 * (1 - x) + core

    barrier = pltpu.get_barrier_semaphore()
    for e in range(1, 4):
        pl.semaphore_signal(
            barrier, inc=1, device_id={"col": lax.rem(k + e, 4)}, device_id_type=MESH
        )
    for d in range(1, nz):
        pl.semaphore_signal(
            barrier, inc=1, device_id={"fib": lax.rem(z + d, nz)}, device_id_type=MESH
        )
    pl.semaphore_wait(barrier, 3 + nz - 1)

    def wait(ref, sem):
        pltpu.make_async_copy(ref, ref, sem).wait()

    def send(src, dst, send_sem, recv_sem, target):
        pltpu.make_async_remote_copy(
            src_ref=src,
            dst_ref=dst,
            send_sem=send_sem,
            recv_sem=recv_sem,
            device_id=target,
            device_id_type=MESH,
        ).start()

    def rows_of(start, size):
        return pl.ds(pl.multiple_of(start, size), size)

    my_j, their_j = rows_of(core * jl, jl), rows_of((1 - core) * jl, jl)

    @pl.loop(0, ni)
    def _(ic):
        chunk = pl.ds(ic * ic_rows, ic_rows)
        for zi in range(nz):
            base = zi * 4 * LANES
            cells = pl.ds(zi * 2 * LANES, 2 * LANES)
            theirs = rows_of(base + (1 - core) * 2 * LANES, 2 * LANES)
            mine = rows_of(base + core * 2 * LANES, 2 * LANES)
            send(
                slab.at[chunk, :, theirs], xcat.at[chunk, my_j, cells],
                core_send.at[ic], core_recv.at[ic], {"col": sibling},
            )
            pltpu.make_async_copy(
                slab.at[chunk, :, mine], xcat.at[chunk, my_j, cells], core_local.at[ic]
            ).start()

    def place(ref, factor):
        high, low = split(factor)
        size, depth = factor.shape
        ref[:size, :depth] = high
        ref[:size, depth:] = high
        ref[size:, :depth] = low
        ref[size:, depth:] = jnp.zeros_like(low)

    place(a2, f2[:, rows_of(x * 2 * jl, 2 * jl)])
    place(a1, f1[...])

    def product(factor, values):
        high, low = split(values)
        both = jnp.dot(
            factor, jnp.concatenate([high, low], axis=0), preferred_element_type=jnp.float32
        )
        half = both.shape[0] // 2
        return both[:half] + both[half:]

    def to_second_rank(ic):
        chunk = pl.ds(ic * ic_rows, ic_rows)
        wait(xcat.at[chunk, my_j], core_local.at[ic])
        wait(xcat.at[chunk, their_j], core_recv.at[ic])

        @pl.loop(0, ic_rows)
        def _(step):
            i = ic * ic_rows + step
            for zi in range(nz):
                part = product(a2[...], xcat[i, :, zi * 2 * LANES : (zi + 1) * 2 * LANES])
                for qc in range(nq):
                    at = slice(qc * qc_rows, (qc + 1) * qc_rows)
                    pb[0, qc, zi, i] = part[at, :LANES]
                    pb[1, qc, zi, i] = part[at, LANES:]

    def send_last(ic):
        chunk = pl.ds(ic * ic_rows, ic_rows)
        for d in range(1, nz):
            peer = lax.rem(z + d, nz)
            send(
                pb.at[:, last, peer, chunk], gf.at[:, z, chunk],
                zf_send.at[d - 1], zf_recv.at[d - 1], {"fib": peer},
            )
        gf[:, z, chunk] = pb[:, last, z, chunk]

    def send_half(s):
        qc, ic = s // ni, lax.rem(s, ni)
        chunk = pl.ds(ic * ic_rows, ic_rows)
        send(
            pb.at[1 - x, qc, :, chunk], xr.at[qc, :, chunk],
            x_send.at[s], x_recv.at[s], {"col": partner},
        )

    def add_and_send(s):
        qc, ic = s // ni, lax.rem(s, ni)
        chunk = pl.ds(ic * ic_rows, ic_rows)
        wait(xr.at[qc, :, chunk], x_recv.at[s])
        for zi in range(nz):
            pb[x, qc, zi, chunk] = pb[x, qc, zi, chunk] + xr[qc, zi, chunk]
        g[qc, z, chunk] = pb[x, qc, z, chunk]
        for d in range(1, nz):
            peer = lax.rem(z + d, nz)
            send(
                pb.at[x, qc, peer, chunk], g.at[qc, z, chunk],
                z_send.at[qc, d - 1], z_recv.at[qc, d - 1], {"fib": peer},
            )

    def sub(column):
        return rows_of((lax.rem(column, 2) * 2 + column // 2) * LANES, LANES)

    def to_first_rank(qc):
        for d in range(1, nz):
            wait(g.at[qc, lax.rem(z - d + nz, nz)], z_recv.at[qc, d - 1])
        flat = g.at[qc].reshape(points * qc_rows, LANES)
        ranked = rr.at[qc].reshape(ranks * qc_rows, LANES)

        @pl.loop(0, qc_rows // 2)
        def _(pair):
            q = 2 * pair
            values = jnp.concatenate(
                [flat[pl.ds(q + t, points, stride=qc_rows), :] for t in range(2)], axis=1
            )
            part = product(a1[...], values)
            for t in range(2):
                ranked[pl.ds(q + t, ranks, stride=qc_rows), :] = part[
                    :, t * LANES : (t + 1) * LANES
                ]

        qs = rows_of(qc * qc_rows, qc_rows)
        for e in range(1, 4):
            peer = lax.rem(k + e, 4)
            send(
                rr.at[qc, pl.ds(peer * own_ranks, own_ranks)], out.at[:, qs, sub(k)],
                o_send.at[qc, e - 1], o_recv.at[qc, e - 1], {"col": peer},
            )
        pltpu.make_async_copy(
            rr.at[qc, pl.ds(k * own_ranks, own_ranks)], out.at[:, qs, sub(k)], o_local.at[qc]
        ).start()

    half = 2 * own_ranks
    my_half, their_half = pl.ds(x * half, half), pl.ds((1 - x) * half, half)
    last_qs = pl.ds(last * qc_rows, qc_rows)

    def last_to_first_rank():
        for d in range(1, nz):
            wait(gf.at[:, lax.rem(z - d + nz, nz)], zf_recv.at[d - 1])
        flats = [gf.at[t].reshape(points * qc_rows, LANES) for t in range(2)]
        ranked = [rf.at[t].reshape(ranks * qc_rows, LANES) for t in range(2)]

        @pl.loop(0, qc_rows)
        def _(q):
            values = jnp.concatenate(
                [flat[pl.ds(q, points, stride=qc_rows), :] for flat in flats], axis=1
            )
            part = product(a1[...], values)
            for t in range(2):
                ranked[t][pl.ds(q, ranks, stride=qc_rows), :] = part[
                    :, t * LANES : (t + 1) * LANES
                ]

        send(rf.at[:, their_half], rx, f_send, f_recv, {"col": partner})

    def last_cells(which, t):
        return rows_of((which * 2 + t) * LANES, LANES)

    def last_out():
        wait(rx, f_recv)
        for t in range(2):
            rx[t] = rx[t] + rf[t, my_half]
            place_at = out.at[:, last_qs, last_cells(core, t)]
            send(
                rx.at[t, pl.ds((1 - core) * own_ranks, own_ranks)], place_at,
                s_send.at[t], s_recv.at[t], {"col": sibling},
            )
            pltpu.make_async_copy(
                rx.at[t, pl.ds(core * own_ranks, own_ranks)], place_at, s_local.at[t]
            ).start()

    steps = last * ni

    @pl.loop(0, steps + LAG)
    def _(s):
        @pl.when(s < ni)
        def _():
            to_second_rank(s)

        @pl.when(s < steps)
        def _():
            send_half(s)

        @pl.when(s < ni)
        def _():
            send_last(s)

        @pl.when(s >= LAG)
        def _():
            add_and_send(s - LAG)

    for qc in range(last):
        to_first_rank(qc)
        if qc == 0:
            last_to_first_rank()
        if qc == 1:
            last_out()

    @pl.loop(0, ni)
    def _(ic):
        chunk = pl.ds(ic * ic_rows, ic_rows)
        wait(xcat.at[chunk, my_j], core_send.at[ic])

    @pl.loop(0, steps)
    def _(s):
        qc, ic = s // ni, lax.rem(s, ni)
        wait(pb.at[1 - x, qc, :, pl.ds(ic * ic_rows, ic_rows)], x_send.at[s])

    for d in range(1, nz):
        wait(pb.at[:, last, lax.rem(z + d, nz)], zf_send.at[d - 1])
    wait(rf.at[:, their_half], f_send)
    for t in range(2):
        wait(rx.at[t, pl.ds((1 - core) * own_ranks, own_ranks)], s_send.at[t])
        wait(out.at[:, last_qs, last_cells(1 - core, t)], s_recv.at[t])
        wait(out.at[:, last_qs, last_cells(core, t)], s_local.at[t])
    for qc in range(last):
        qs = pl.ds(qc * qc_rows, qc_rows)
        for d in range(1, nz):
            wait(pb.at[x, qc, lax.rem(z + d, nz)], z_send.at[qc, d - 1])
        for e in range(1, 4):
            wait(rr.at[qc, pl.ds(lax.rem(k + e, 4) * own_ranks, own_ranks)], o_send.at[qc, e - 1])
            wait(out.at[:, qs, sub(lax.rem(k - e + 4, 4))], o_recv.at[qc, e - 1])
        wait(out.at[:, qs, sub(k)], o_local.at[qc])


def fused(nz, data_slab, first_factor, second_factor):
    rows, jl, cells = data_slab.shape
    ranks, qs = first_factor.shape[1], second_factor.shape[1]
    nq, ni = Q_CHUNKS, I_CHUNKS
    qc_rows = qs // nq
    f32, bf16 = jnp.float32, jnp.bfloat16
    dma = pltpu.SemaphoreType.DMA
    last = nq - 1
    scratch = [
        pltpu.VMEM((rows, 2 * jl, cells // 2), f32),
        pltpu.VMEM((2, nq, nz, rows, qc_rows, LANES), f32),
        pltpu.VMEM((last, nz, rows, qc_rows, LANES), f32),
        pltpu.VMEM((last, nz, rows, qc_rows, LANES), f32),
        pltpu.VMEM((2, nz, rows, qc_rows, LANES), f32),
        pltpu.VMEM((last, ranks, qc_rows, LANES), f32),
        pltpu.VMEM((2, ranks, qc_rows, LANES), f32),
        pltpu.VMEM((2, ranks // 2, qc_rows, LANES), f32),
        pltpu.VMEM((2 * ranks, 2 * nz * rows), bf16),
        pltpu.VMEM((2 * qs, 4 * jl), bf16),
        dma((ni,)), dma((ni,)), dma((ni,)),
        dma((last * ni,)), dma((last * ni,)),
        dma((last, nz - 1)), dma((last, nz - 1)),
        dma((nz - 1,)), dma((nz - 1,)),
        dma((last, 3)), dma((last, 3)), dma((last,)),
        dma, dma,
        dma((2,)), dma((2,)), dma((2,)),
    ]
    return pl.pallas_call(
        functools.partial(kernel, nz, nq, ni),
        out_shape=jax.ShapeDtypeStruct((ranks // 4, qs, cells // nz), f32),
        in_specs=[
            pl.BlockSpec(memory_space=pl.ANY),
            pl.BlockSpec(memory_space=pltpu.VMEM),
            pl.BlockSpec(memory_space=pltpu.VMEM),
        ],
        out_specs=pl.BlockSpec(memory_space=pl.ANY),
        scratch_shapes=scratch,
        compiler_params=pltpu.CompilerParams(
            collective_id=0, has_side_effects=True, vmem_limit_bytes=VMEM_MIB * 1024 * 1024
        ),
    )(data_slab, first_factor.T, second_factor.T)


def solution(mesh):
    nz, nc = mesh.shape["fib"], mesh.shape["col"]

    def on_each(data_slab, first_factor, second_factor):
        cells = data_slab.shape[2]
        if nc == 4 and nz > 1 and cells == nz * nc * LANES:
            return fused(nz, data_slab, first_factor, second_factor)
        return on_device(data_slab, first_factor, second_factor)

    in_specs = (P(("groups", "fib"), "col", None), P(), P())
    out_specs = P(("groups", "col"), None, "fib")
    return jax.shard_map(
        on_each, mesh=mesh, in_specs=in_specs, out_specs=out_specs, check_vma=False
    )
```

time: 218 us -> 196 us (0.90)
  Pallas kernels: 209 us -> 189 us
    pallas_call x1, Pallas kernels: 209 us -> 189 us  [fused(): pl.pallas_call(functools.partial(kernel, nz, nq, ni), out_shape=jax.Shape...]
    unnamed x3 -> x5, local copies, waits for them, and re-layouts: 8.46 us -> 6.99 us
where the time goes in v2:
time: 196 us
  Pallas kernels  189 us (96%)
  local copies, waits for them, and re-layouts  6.99 us (4%)
    pallas_call x1, Pallas kernels, fused(): pl.pallas_call(functools.partial(kernel, nz, nq, ni), out_shape=jax.Shape...  189 us
    unnamed x5, local copies, waits for them, and re-layouts  6.99 us

profile of v2, /device:TPU:1, one launch (start us, length us, event | category | flops | bytes accessed | tf_op | source)
XLA Modules:
  0.0 195.9 jit_solution(3219605038673745193)
XLA Ops:
  0.0 0.0 copy-start
  0.0 0.9 copy-done
  0.9 0.0 copy-start.1
  0.9 0.8 copy-done.1
  1.7 188.9 %shard_map.37 = f32[24,96,512]{2,1,0:T(8,128)} custom-call(f32[32,64,2048]{2,1,0:T(8,128)} %slab.1, f32[96,128]{1,0:T(8,128)S(1)} %bitcast.3, f32[96,256]{1,0:T(8,128)S(1)} %bitcast.2), custom_call_target="tpu_custom_call" | custom-call | tf_op jit(solution)/shard_map/pallas_call | solution.py:322
  190.6 5.3 %copy.5 = f32[24,96,512]{2,1,0:T(8,128)} copy(f32[24,96,512]{2,1,0:T(8,128)} %shard_map.37) | data formatting | bytes 9437184
Async XLA Ops:
  0.0 0.9 copy-start
  0.9 0.8 copy-start.1

commit v3 on v2

--- a/solution.py
+++ b/solution.py
@@ -10,9 +10,12 @@
 MESH = pl.DeviceIdType.MESH
 LANES = 128
 Q_CHUNKS = 6
-I_CHUNKS = 4
-LAG = 2
-VMEM_MIB = 50
+I_CHUNKS = 8
+LAG = 4
+F_AT = 1
+OUT_AT = 2
+ORDER = (2, 3, 1)
+VMEM_MIB = 48
 
 
 def second_mode(first_core, second_factor):
@@ -30,6 +33,10 @@
         "ir,ijc->rjc", first_factor, moved_slab, precision=lax.Precision.HIGHEST
     )
     return second_mode(first_core, second_factor)
+
+
+def swapped(z, d):
+    return {1: z + 1 - 2 * lax.rem(z, 2), 2: lax.rem(z + 2, 4), 3: 3 - z}[d]
 
 
 def split(values):
@@ -63,7 +70,7 @@
         )
     for d in range(1, nz):
         pl.semaphore_signal(
-            barrier, inc=1, device_id={"fib": lax.rem(z + d, nz)}, device_id_type=MESH
+            barrier, inc=1, device_id={"fib": swapped(z, d)}, device_id_type=MESH
         )
     pl.semaphore_wait(barrier, 3 + nz - 1)
 
@@ -137,8 +144,8 @@
 
     def send_last(ic):
         chunk = pl.ds(ic * ic_rows, ic_rows)
-        for d in range(1, nz):
-            peer = lax.rem(z + d, nz)
+        for d in ORDER:
+            peer = swapped(z, d)
             send(
                 pb.at[:, last, peer, chunk], gf.at[:, z, chunk],
                 zf_send.at[d - 1], zf_recv.at[d - 1], {"fib": peer},
@@ -160,8 +167,8 @@
         for zi in range(nz):
             pb[x, qc, zi, chunk] = pb[x, qc, zi, chunk] + xr[qc, zi, chunk]
         g[qc, z, chunk] = pb[x, qc, z, chunk]
-        for d in range(1, nz):
-            peer = lax.rem(z + d, nz)
+        for d in ORDER:
+            peer = swapped(z, d)
             send(
                 pb.at[x, qc, peer, chunk], g.at[qc, z, chunk],
                 z_send.at[qc, d - 1], z_recv.at[qc, d - 1], {"fib": peer},
@@ -172,7 +179,7 @@
 
     def to_first_rank(qc):
         for d in range(1, nz):
-            wait(g.at[qc, lax.rem(z - d + nz, nz)], z_recv.at[qc, d - 1])
+            wait(g.at[qc, swapped(z, d)], z_recv.at[qc, d - 1])
         flat = g.at[qc].reshape(points * qc_rows, LANES)
         ranked = rr.at[qc].reshape(ranks * qc_rows, LANES)
 
@@ -205,7 +212,7 @@
 
     def last_to_first_rank():
         for d in range(1, nz):
-            wait(gf.at[:, lax.rem(z - d + nz, nz)], zf_recv.at[d - 1])
+            wait(gf.at[:, swapped(z, d)], zf_recv.at[d - 1])
         flats = [gf.at[t].reshape(points * qc_rows, LANES) for t in range(2)]
         ranked = [rf.at[t].reshape(ranks * qc_rows, LANES) for t in range(2)]
 
@@ -258,12 +265,11 @@
         def _():
             add_and_send(s - LAG)
 
-    for qc in range(last):
-        to_first_rank(qc)
-        if qc == 0:
-            last_to_first_rank()
-        if qc == 1:
-            last_out()
+    pl.loop(0, F_AT)(to_first_rank)
+    last_to_first_rank()
+    pl.loop(F_AT, OUT_AT)(to_first_rank)
+    last_out()
+    pl.loop(OUT_AT, last)(to_first_rank)
 
     @pl.loop(0, ni)
     def _(ic):
@@ -276,7 +282,7 @@
         wait(pb.at[1 - x, qc, :, pl.ds(ic * ic_rows, ic_rows)], x_send.at[s])
 
     for d in range(1, nz):
-        wait(pb.at[:, last, lax.rem(z + d, nz)], zf_send.at[d - 1])
+        wait(pb.at[:, last, swapped(z, d)], zf_send.at[d - 1])
     wait(rf.at[:, their_half], f_send)
     for t in range(2):
         wait(rx.at[t, pl.ds((1 - core) * own_ranks, own_ranks)], s_send.at[t])
@@ -285,7 +291,7 @@
     for qc in range(last):
         qs = pl.ds(qc * qc_rows, qc_rows)
         for d in range(1, nz):
-            wait(pb.at[x, qc, lax.rem(z + d, nz)], z_send.at[qc, d - 1])
+            wait(pb.at[x, qc, swapped(z, d)], z_send.at[qc, d - 1])
         for e in range(1, 4):
             wait(rr.at[qc, pl.ds(lax.rem(k + e, 4) * own_ranks, own_ranks)], o_send.at[qc, e - 1])
             wait(out.at[:, qs, sub(lax.rem(k - e + 4, 4))], o_recv.at[qc, e - 1])
@@ -340,7 +346,7 @@
 
     def on_each(data_slab, first_factor, second_factor):
         cells = data_slab.shape[2]
-        if nc == 4 and nz > 1 and cells == nz * nc * LANES:
+        if nc == 4 and nz == 4 and cells == nz * nc * LANES:
             return fused(nz, data_slab, first_factor, second_factor)
         return on_device(data_slab, first_factor, second_factor)
 

time: 196 us -> 191 us (0.974)
  local copies, waits for them, and re-layouts: 6.99 us -> 3.88 us
  Pallas kernels: 189 us -> 187 us
    unnamed x5, local copies, waits for them, and re-layouts: 6.99 us -> 3.88 us
    pallas_call x1, Pallas kernels: 189 us -> 187 us  [fused(): pl.pallas_call(functools.partial(kernel, nz, nq, ni), out_shape=jax.Shape...]
where the time goes in v3:
time: 191 us
  Pallas kernels  187 us (98%)
  local copies, waits for them, and re-layouts  3.88 us (2%)
    pallas_call x1, Pallas kernels, fused(): pl.pallas_call(functools.partial(kernel, nz, nq, ni), out_shape=jax.Shape...  187 us
    unnamed x5, local copies, waits for them, and re-layouts  3.88 us

profile of v3, /device:TPU:1, one launch (start us, length us, event | category | flops | bytes accessed | tf_op | source)
XLA Modules:
  0.0 190.5 jit_solution(5949046286086017336)
XLA Ops:
  0.0 0.0 copy-start
  0.0 0.9 copy-done
  0.9 0.0 copy-start.1
  0.9 0.8 copy-done.1
  1.7 186.7 %shard_map.37 = f32[24,96,512]{2,1,0:T(8,128)S(1)} custom-call(f32[32,64,2048]{2,1,0:T(8,128)} %slab.1, f32[96,128]{1,0:T(8,128)S(1)} %bitcast.3, f32[96,256]{1,0:T(8,128)S(1)} %bitcast.2), custom_call_target="tpu_custom_call" | custom-call | tf_op jit(solution)/shard_map/pallas_call | solution.py:328
  188.4 2.2 %copy.5 = f32[24,96,512]{2,1,0:T(8,128)} copy(f32[24,96,512]{2,1,0:T(8,128)S(1)} %shard_map.37) | data formatting | bytes 9437184
Async XLA Ops:
  0.0 0.9 copy-start
  0.9 0.8 copy-start.1
